TPU v7x, 32 devices: a whole 2x2x4 slice. The times are simulated.
32 devices in a mesh: groups: 2 (over y), fsdp: 8 (over z, x), dp: 1, sub: 2 (over core).
Axes of the slice: x: 2, y: 2, z: 4, core: 2. Of those that a mesh axis runs over, the one named last changes fastest.
Arguments:
- features: bfloat16 [16, 768, 1280], P(('groups', 'fsdp', 'dp'), 'sub'), parts along dimension 0, may hold values from -6 to 6
- golden: bfloat16 [4, 768, 1280], P(('groups', 'dp'), 'sub'), parts along dimension 0, may hold values from -6 to 6
- die_wafer: int32 [16], P(('groups', 'fsdp', 'dp')), parts along dimension 0, may hold values from 0 to 1
- norm_gain: float32 [1280], replicated, may hold values from 0.1 to 1.9
- proj_weight: bfloat16 [1280, 2560], P('fsdp'), may hold values from -0.15625 to 0.15625
- out_weight: bfloat16 [2560, 1280], P('fsdp'), may hold values from -0.125 to 0.125
- zero_weight: bfloat16 [1280, 1280], P(None, 'fsdp'), may hold values from -0.15625 to 0.15625
Outputs:
- block_out: bfloat16 [16, 768, 1280], P(('groups', 'fsdp', 'dp'), 'sub'), parts along dimension 0
There are 2 independent parts, one for each index of `groups`. A program takes and returns all parts, laid end to end along the dimension named above; an argument that names none is the same for every part. Nothing has to cross between parts.
All inputs are finite; a program needn't handle non-finite values.
Results may differ from a plain program's by a relative error of at most 0.005.
Values may be sent and summed in bfloat16 or wider, within the bound.
A program may use at most 128 MiB of HBM per device.

v0:
```python
import jax
import jax.numpy as jnp
from jax import lax
from jax.sharding import PartitionSpec as P


def body(features, golden, die_wafer, norm_gain, proj_weight, out_weight, zero_weight):
    wafer_one = die_wafer[0]
    columns = jnp.einsum(
        "wpc,cd->wpd", golden, zero_weight, preferred_element_type=jnp.float32
    ).astype(jnp.bfloat16)
    gathered = lax.all_gather(columns, "fsdp", axis=2, tiled=True)
    residual = lax.dynamic_index_in_dim(gathered, wafer_one, 0, keepdims=False)
    mixed = features[0].astype(jnp.float32) + residual.astype(jnp.float32)
    average = jnp.mean(mixed, axis=-1, keepdims=True)
    centred = mixed - average
    variance = jnp.mean(centred * centred, axis=-1, keepdims=True)
    normed = (centred * lax.rsqrt(variance + 1e-05) * norm_gain).astype(jnp.bfloat16)
    inputs = normed
    preact = jnp.dot(
        inputs,
        lax.all_gather(proj_weight, "fsdp", axis=0, tiled=True),
        preferred_element_type=jnp.float32,
    )
    hidden = jax.nn.gelu(preact, approximate=True).astype(jnp.bfloat16)
    inputs = hidden
    branch = jnp.dot(
        inputs,
        lax.all_gather(out_weight, "fsdp", axis=0, tiled=True),
        preferred_element_type=jnp.float32,
    )
    return (mixed + branch).astype(jnp.bfloat16)[None]


def solution(mesh):
    placed = (
        P(("groups", "fsdp", "dp"), "sub", None),
        P(("groups", "dp"), "sub", None),
        P(("groups", "fsdp", "dp")),
        P(),
        P("fsdp", None),
        P("fsdp", None),
        P(None, "fsdp"),
    )
    return jax.shard_map(
        body,
        mesh=mesh,
        in_specs=placed,
        out_specs=P(("groups", "fsdp", "dp"), "sub", None),
        check_vma=False,
    )
```

profile of v0, /device:TPU:0, one launch (start us, length us, event | category | flops | bytes accessed | tf_op | source)
XLA Modules:
  0.0 289.0 jit_solution(17761163579044327469)
XLA Ops:
  6.5 0.0 copy-start
  6.5 0.0 all-gather.4.cloned.1.call-start
  6.5 1.5 copy-done
  8.1 2.5 convolution_convert_fusion
  10.6 0.0 all-gather.4.cloned.1.call-update
  10.6 0.0 all-gather.6.cloned.1.call-start
  10.7 0.7 all-gather.6.cloned.1.call-update
  11.4 0.0 all-gather.8.cloned.1.call-start
  11.4 0.7 all-gather.8.cloned.1.call-update
  12.7 1.6 copy.8
  14.3 46.6 %all-gather.4.cloned.1.call-done = bf16[2,384,1280]{1,2,0:T(8,128)(2,1)} async-done(((bf16[2,384,160]{1,2,0:T(8,128)(2,1)}), bf16[2,384,1280]{1,2,0:T(8,128)(2,1)}) %all-gather.4.cloned.1.call-update) | async-done | bytes 1966096 | tf_op jit(solution)/shard_map/all_gather | solution.py:12
  61.0 0.0 copy-start.1
  61.0 0.0 copy-start.2
  61.0 1.7 fusion.15
  62.7 0.1 copy-done.1
  62.8 0.4 multiply_reduce_fusion
  63.3 101.3 %all-gather.6.cloned.1.call-done = bf16[1280,2560]{1,0:T(8,128)(2,1)} async-done(((bf16[160,2560]{1,0:T(8,128)(2,1)}), bf16[1280,2560]{1,0:T(8,128)(2,1)}) %all-gather.6.cloned.1.call-update) | async-done | bytes 6553616 | tf_op jit(solution)/shard_map/all_gather | solution.py:22
  164.5 102.6 %all-gather.8.cloned.1.call-done = bf16[2560,1280]{1,0:T(8,128)(2,1)} async-done(((bf16[320,1280]{1,0:T(8,128)(2,1)}), bf16[2560,1280]{1,0:T(8,128)(2,1)}) %all-gather.8.cloned.1.call-update) | async-done | bytes 6553616 | tf_op jit(solution)/shard_map/all_gather | solution.py:29
  267.2 0.0 copy-done.2
  267.2 13.0 %fusion.9 = bf16[1,384,1280]{1,2,0:T(8,128)(2,1)} fusion(bf16[2560,1280]{1,0:T(8,128)(2,1)} %all-gather.8.cloned.1.call-done, bf16[1,384,1280]{1,2,0:T(8,128)(2,1)S(1)} %copy.8, bf16[1280,2560]{1,0:T(8,128)(2,1)} %all-gather.6.cloned.1.call-done, f32[1280]{0:T(1024)S(1)} %copy-done.2, f32[384]{0:T(512)S(1)} %add_rsqrt_fusion, ...), kind=kOutput, calls=%fused_computation.11 | convolution fusion | flops 5047910400 | bytes 18035712 | tf_op jit(solution)/shard_map/dot_general | solution.py:27
  280.2 2.2 copy.10
  (2 shorter events, 0.0 us)
Async XLA Ops:
  6.5 1.5 copy-start
  6.5 54.4 %all-gather.4.cloned.1.call-start = ((), (), s32[]{:S(2)}) async-start(), calls=%async_computation | async-start | bytes 2211840 | tf_op jit(solution)/shard_map/all_gather | solution.py:12
  10.6 153.9 %all-gather.6.cloned.1.call-start = ((), (), s32[]{:S(2)}) async-start(), calls=%async_computation.1 | async-start | bytes 7372800 | tf_op jit(solution)/shard_map/all_gather | solution.py:22
  11.4 255.8 %all-gather.8.cloned.1.call-start = ((), (), s32[]{:S(2)}) async-start(), calls=%async_computation.2 | async-start | bytes 7372800 | tf_op jit(solution)/shard_map/all_gather | solution.py:29
  61.0 1.8 copy-start.1
  61.0 206.2 %copy-start.2 = (f32[1280]{0:T(1024)S(1)}, f32[1280]{0:T(1024)}, u32[]{:S(2)}) copy-start(f32[1280]{0:T(1024)} %param.10) | copy-start | bytes 15364
Sparse Core Ops, SparseCore 0:
  10.7 50.2 all-gather.3
  63.2 101.3 all-gather.5
  166.7 100.3 all-gather.7
where the time goes:
time: 289 us
  waiting for transfers between devices  252 us (87%)
  matrix products  15.5 us (5%)
  between operations  13.8 us (5%)
  local copies, waits for them, and re-layouts  5.51 us (2%)
    all_gather x1, waiting for transfers between devices, body(): lax.all_gather(out_weight, 'fsdp', axis=0, tiled=True)  103 us
    all_gather x1, waiting for transfers between devices, body(): lax.all_gather(proj_weight, 'fsdp', axis=0, tiled=True)  101 us
    all_gather x1, waiting for transfers between devices, body(): gathered = lax.all_gather(columns, 'fsdp', axis=2, tiled=True)  46.6 us
    dot_general x1, matrix products, body(): jnp.dot(inputs, lax.all_gather(out_weight, 'fsdp', axis=0, tiled=True), p...  13 us
  transfers between devices with their start and end apart: 3, of which 3 were waited for; matrix products, arithmetic and copies ran while one was open for 1% of the time, Pallas kernels for 0%

commit v1 on v0

--- a/solution.py
+++ b/solution.py
@@ -9,7 +9,23 @@
     columns = jnp.einsum(
         "wpc,cd->wpd", golden, zero_weight, preferred_element_type=jnp.float32
     ).astype(jnp.bfloat16)
-    gathered = lax.all_gather(columns, "fsdp", axis=2, tiled=True)
+
+    def make_spans(array_here, named_axis):
+        n_slots = lax.axis_size(named_axis)
+        items = [(idx, (idx + 1) % n_slots) for idx in range(n_slots)]
+
+        def note_the_threads(f_next):
+            if len(f_next) == n_slots:
+                return f_next
+            found_now = lax.ppermute(f_next[0], perm=items, axis_name=named_axis)
+            return note_the_threads([found_now, *f_next])
+
+        reached = note_the_threads([array_here])
+        near = jnp.concatenate(reached, axis=2)
+        row_out = lax.axis_index(named_axis)
+        return jnp.roll(near, (row_out + 1) * array_here.shape[2], axis=2)
+
+    gathered = make_spans(columns, "fsdp")
     residual = lax.dynamic_index_in_dim(gathered, wafer_one, 0, keepdims=False)
     mixed = features[0].astype(jnp.float32) + residual.astype(jnp.float32)
     average = jnp.mean(mixed, axis=-1, keepdims=True)

time: 289 us -> 269 us (0.931)
  waiting for transfers between devices: 252 us -> 219 us
  local copies, waits for them, and re-layouts: 5.51 us -> 16.3 us
  starting transfers between devices: 0.08 us -> 3.05 us
    ppermute x0 -> x7, waiting for transfers between devices: none -> 96.8 us  [note_the_threads(): found_now = lax.ppermute(f_next[0], perm=items, axis_name=named_axis)]
    all_gather x1, waiting for transfers between devices: 101 us -> 16.3 us  [body(): lax.all_gather(proj_weight, 'fsdp', axis=0, tiled=True)]
    all_gather x1 -> x0, waiting for transfers between devices: 46.6 us -> none  [body(): gathered = lax.all_gather(columns, 'fsdp', axis=2, tiled=True)]
    unnamed x7 -> x38, local copies, waits for them, and re-layouts: 3.28 us -> 14 us
    ppermute x0 -> x7, starting transfers between devices: none -> 3.01 us  [note_the_threads(): found_now = lax.ppermute(f_next[0], perm=items, axis_name=named_axis)]
  transfers between devices with their start and end apart: 3 -> 9, of which waited for: 3 -> 9; matrix products, arithmetic and copies ran while one was open for 1% -> 5% of each run, Pallas kernels for 0% -> 0%
where the time goes in v1:
time: 269 us; the launch traced here: 268 us
  waiting for transfers between devices  219 us (81%)
  local copies, waits for them, and re-layouts  16.3 us (6%)
  matrix products  15 us (6%)
  between operations  14.3 us (5%)
  starting transfers between devices  3.05 us (1%)
    all_gather x1, waiting for transfers between devices, body(): lax.all_gather(out_weight, 'fsdp', axis=0, tiled=True)  104 us
    ppermute x7, waiting for transfers between devices, note_the_threads(): found_now = lax.ppermute(f_next[0], perm=items, axis_name=named_axis)  96.8 us
    all_gather x1, waiting for transfers between devices, body(): lax.all_gather(proj_weight, 'fsdp', axis=0, tiled=True)  16.3 us
    unnamed x38, local copies, waits for them, and re-layouts  14 us
    dot_general x1, matrix products, body(): jnp.dot(inputs, lax.all_gather(out_weight, 'fsdp', axis=0, tiled=True), p...  13.2 us
  transfers between devices with their start and end apart: 9, of which 9 were waited for; matrix products, arithmetic and copies ran while one was open for 5% of the time, Pallas kernels for 0%

profile of v1, /device:TPU:0, one launch (start us, length us, event | category | flops | bytes accessed | tf_op | source)
XLA Modules:
  0.0 268.1 jit_solution(14644195445013580783)
XLA Ops:
  6.5 0.7 all-gather.3.cloned.1.call-update
  8.1 1.8 convolution_convert_fusion
  9.9 3.0 %collective-permute-start = (bf16[2,384,160]{1,2,0:T(8,128)(2,1)S(1)}, bf16[2,384,160]{1,2,0:T(8,128)(2,1)S(1)}, u32[]{:S(2)}, u32[]{:S(2)}) collective-permute-start(bf16[2,384,160]{1,2,0:T(8,128)(2,1)S(1)} %convolution_convert_fusion), channel_id=1, source_target_pairs={{0,2},{2,4},{4,6},{6,8},{8,10},{10,12},{12,14},{14,0},{1,3},{3,5},... | collective-permute-start | bytes 737288 | tf_op jit(solution)/shard_map/ppermute | solution.py:20
  12.9 9.0 %collective-permute-done = bf16[2,384,160]{1,2,0:T(8,128)(2,1)S(1)} collective-permute-done((bf16[2,384,160]{1,2,0:T(8,128)(2,1)S(1)}, bf16[2,384,160]{1,2,0:T(8,128)(2,1)S(1)}, u32[]{:S(2)}, u32[]{:S(2)}) %collective-permute-start) | collective-permute-done | bytes 245792 | tf_op jit(solution)/shard_map/ppermute | solution.py:20
  21.9 16.2 %collective-permute-done.1 = bf16[2,384,160]{1,2,0:T(8,128)(2,1)S(1)} collective-permute-done((bf16[2,384,160]{1,2,0:T(8,128)(2,1)S(1)}, bf16[2,384,160]{1,2,0:T(8,128)(2,1)S(1)}, u32[]{:S(2)}, u32[]{:S(2)}) %collective-permute-start.1) | collective-permute-done | bytes 245792 | tf_op jit(solution)/shard_map/ppermute | solution.py:20
  38.7 15.9 %collective-permute-done.2 = bf16[2,384,160]{1,2,0:T(8,128)(2,1)S(1)} collective-permute-done((bf16[2,384,160]{1,2,0:T(8,128)(2,1)S(1)}, bf16[2,384,160]{1,2,0:T(8,128)(2,1)S(1)}, u32[]{:S(2)}, u32[]{:S(2)}) %collective-permute-start.2) | collective-permute-done | bytes 245792 | tf_op jit(solution)/shard_map/ppermute | solution.py:20
  55.4 13.3 %collective-permute-done.3 = bf16[2,384,160]{1,2,0:T(8,128)(2,1)S(1)} collective-permute-done((bf16[2,384,160]{1,2,0:T(8,128)(2,1)S(1)}, bf16[2,384,160]{1,2,0:T(8,128)(2,1)S(1)}, u32[]{:S(2)}, u32[]{:S(2)}) %collective-permute-start.3) | collective-permute-done | bytes 245792 | tf_op jit(solution)/shard_map/ppermute | solution.py:20
  69.3 14.9 %collective-permute-done.4 = bf16[2,384,160]{1,2,0:T(8,128)(2,1)S(1)} collective-permute-done((bf16[2,384,160]{1,2,0:T(8,128)(2,1)S(1)}, bf16[2,384,160]{1,2,0:T(8,128)(2,1)S(1)}, u32[]{:S(2)}, u32[]{:S(2)}) %collective-permute-start.4) | collective-permute-done | bytes 245792 | tf_op jit(solution)/shard_map/ppermute | solution.py:20
  85.0 15.0 %collective-permute-done.5 = bf16[2,384,160]{1,2,0:T(8,128)(2,1)} collective-permute-done((bf16[2,384,160]{1,2,0:T(8,128)(2,1)S(1)}, bf16[2,384,160]{1,2,0:T(8,128)(2,1)}, u32[]{:S(2)}, u32[]{:S(2)}) %collective-permute-start.5) | collective-permute-done | bytes 245792 | tf_op jit(solution)/shard_map/ppermute | solution.py:20
  100.6 1.6 copy.8
  102.2 12.6 %collective-permute-done.6 = bf16[2,384,160]{1,2,0:T(8,128)(2,1)} collective-permute-done((bf16[2,384,160]{1,2,0:T(8,128)(2,1)}, bf16[2,384,160]{1,2,0:T(8,128)(2,1)}, u32[]{:S(2)}, u32[]{:S(2)}) %collective-permute-start.6) | collective-permute-done | bytes 245792 | tf_op jit(solution)/shard_map/ppermute | solution.py:20
  114.8 1.0 constant_dynamic-update-slice_fusion.15
  115.8 1.0 constant_dynamic-update-slice_fusion.14
  116.7 1.0 constant_dynamic-update-slice_fusion.13
  117.7 1.0 constant_dynamic-update-slice_fusion.12
  118.7 1.0 constant_dynamic-update-slice_fusion.11
  119.7 1.0 constant_dynamic-update-slice_fusion.10
  120.8 1.0 constant_dynamic-update-slice_fusion.7
  121.8 1.0 constant_dynamic-update-slice_fusion.6
  123.6 1.4 copy-done.1
  125.5 16.3 %all-gather.3.cloned.1.call-done = bf16[1280,2560]{1,0:T(8,128)(2,1)} async-done(((bf16[160,2560]{1,0:T(8,128)(2,1)}), bf16[1280,2560]{1,0:T(8,128)(2,1)}) %all-gather.3.cloned.1.call-update) | async-done | bytes 6553616 | tf_op jit(solution)/shard_map/all_gather | solution.py:38
  141.8 104.0 %all-gather.5.cloned.1.call-done = bf16[2560,1280]{1,0:T(8,128)(2,1)} async-done(((bf16[320,1280]{1,0:T(8,128)(2,1)}), bf16[2560,1280]{1,0:T(8,128)(2,1)}) %all-gather.5.cloned.1.call-update) | async-done | bytes 6553616 | tf_op jit(solution)/shard_map/all_gather | solution.py:45
  245.8 13.2 %fusion.9 = bf16[1,384,1280]{1,2,0:T(8,128)(2,1)} fusion(bf16[2560,1280]{1,0:T(8,128)(2,1)} %all-gather.5.cloned.1.call-done, bf16[1,384,1280]{1,2,0:T(8,128)(2,1)S(1)} %copy.8, bf16[1280,2560]{1,0:T(8,128)(2,1)} %all-gather.3.cloned.1.call-done, f32[1280]{0:T(1024)S(1)} %copy-done.10, f32[384]{0:T(512)S(1)} %add_rsqrt_fusion, ...), kind=kOutput, calls=%fused_computation.11 | convolution fusion | flops 5047910400 | bytes 18036736 | tf_op jit(solution)/shard_map/dot_general | solution.py:43
  259.0 2.2 copy.10
  (42 shorter events, 4.9 us)
Async XLA Ops:
  6.5 1.5 copy-start
  6.5 135.3 %all-gather.3.cloned.1.call-start = ((), (), s32[]{:S(2)}) async-start(), calls=%async_computation | async-start | bytes 7372800 | tf_op jit(solution)/shard_map/all_gather | solution.py:38
  7.3 238.6 %all-gather.5.cloned.1.call-start = ((), (), s32[]{:S(2)}) async-start(), calls=%async_computation.1 | async-start | bytes 7372800 | tf_op jit(solution)/shard_map/all_gather | solution.py:45
  9.9 12.0 %collective-permute-start = (bf16[2,384,160]{1,2,0:T(8,128)(2,1)S(1)}, bf16[2,384,160]{1,2,0:T(8,128)(2,1)S(1)}, u32[]{:S(2)}, u32[]{:S(2)}) collective-permute-start(bf16[2,384,160]{1,2,0:T(8,128)(2,1)S(1)} %convolution_convert_fusion), channel_id=1, source_target_pairs={{0,2},{2,4},{4,6},{6,8},{8,10},{10,12},{12,14},{14,0},{1,3},{3,5},... | collective-permute-start | bytes 737288 | tf_op jit(solution)/shard_map/ppermute | solution.py:20
  21.9 16.2 %collective-permute-start.1 = (bf16[2,384,160]{1,2,0:T(8,128)(2,1)S(1)}, bf16[2,384,160]{1,2,0:T(8,128)(2,1)S(1)}, u32[]{:S(2)}, u32[]{:S(2)}) collective-permute-start(bf16[2,384,160]{1,2,0:T(8,128)(2,1)S(1)} %collective-permute-done), channel_id=1, source_target_pairs={{0,2},{2,4},{4,6},{6,8},{8,10},{10,12},{12,14},{14,0},{1,3},{3,5},... | collective-permute-start | bytes 737288 | tf_op jit(solution)/shard_map/ppermute | solution.py:20
  38.0 0.7 copy-start.2
  38.7 15.9 %collective-permute-start.2 = (bf16[2,384,160]{1,2,0:T(8,128)(2,1)S(1)}, bf16[2,384,160]{1,2,0:T(8,128)(2,1)S(1)}, u32[]{:S(2)}, u32[]{:S(2)}) collective-permute-start(bf16[2,384,160]{1,2,0:T(8,128)(2,1)S(1)} %collective-permute-done.1), channel_id=1, source_target_pairs={{0,2},{2,4},{4,6},{6,8},{8,10},{10,12},{12,14},{14,0},{1,3},{3,5},... | collective-permute-start | bytes 737288 | tf_op jit(solution)/shard_map/ppermute | solution.py:20
  54.7 0.7 copy-start.4
  55.4 13.3 %collective-permute-start.3 = (bf16[2,384,160]{1,2,0:T(8,128)(2,1)S(1)}, bf16[2,384,160]{1,2,0:T(8,128)(2,1)S(1)}, u32[]{:S(2)}, u32[]{:S(2)}) collective-permute-start(bf16[2,384,160]{1,2,0:T(8,128)(2,1)S(1)} %collective-permute-done.2), channel_id=1, source_target_pairs={{0,2},{2,4},{4,6},{6,8},{8,10},{10,12},{12,14},{14,0},{1,3},{3,5},... | collective-permute-start | bytes 737288 | tf_op jit(solution)/shard_map/ppermute | solution.py:20
  68.6 0.7 copy-start.6
  69.3 14.9 %collective-permute-start.4 = (bf16[2,384,160]{1,2,0:T(8,128)(2,1)S(1)}, bf16[2,384,160]{1,2,0:T(8,128)(2,1)S(1)}, u32[]{:S(2)}, u32[]{:S(2)}) collective-permute-start(bf16[2,384,160]{1,2,0:T(8,128)(2,1)S(1)} %collective-permute-done.3), channel_id=1, source_target_pairs={{0,2},{2,4},{4,6},{6,8},{8,10},{10,12},{12,14},{14,0},{1,3},{3,5},... | collective-permute-start | bytes 737288 | tf_op jit(solution)/shard_map/ppermute | solution.py:20
  84.3 0.7 copy-start.8
  85.0 15.0 %collective-permute-start.5 = (bf16[2,384,160]{1,2,0:T(8,128)(2,1)S(1)}, bf16[2,384,160]{1,2,0:T(8,128)(2,1)}, u32[]{:S(2)}, u32[]{:S(2)}) collective-permute-start(bf16[2,384,160]{1,2,0:T(8,128)(2,1)S(1)} %collective-permute-done.4), channel_id=1, source_target_pairs={{0,2},{2,4},{4,6},{6,8},{8,10},{10,12},{12,14},{14,0},{1,3},{3,5},... | collective-permute-start | bytes 737288 | tf_op jit(solution)/shard_map/ppermute | solution.py:20
  99.9 14.8 %collective-permute-start.6 = (bf16[2,384,160]{1,2,0:T(8,128)(2,1)}, bf16[2,384,160]{1,2,0:T(8,128)(2,1)}, u32[]{:S(2)}, u32[]{:S(2)}) collective-permute-start(bf16[2,384,160]{1,2,0:T(8,128)(2,1)} %collective-permute-done.5), channel_id=1, source_target_pairs={{0,2},{2,4},{4,6},{6,8},{8,10},{10,12},{12,14},{14,0},{1,3},{3,5},... | collective-permute-start | bytes 737288 | tf_op jit(solution)/shard_map/ppermute | solution.py:20
  102.2 20.6 %copy-start.9 = (bf16[2,384,160]{1,2,0:T(8,128)(2,1)S(1)}, bf16[2,384,160]{1,2,0:T(8,128)(2,1)}, u32[]{:S(2)}) copy-start(bf16[2,384,160]{1,2,0:T(8,128)(2,1)} %copy-done.8) | copy-start | bytes 737284
  102.2 20.7 %copy-start.7 = (bf16[2,384,160]{1,2,0:T(8,128)(2,1)S(1)}, bf16[2,384,160]{1,2,0:T(8,128)(2,1)}, u32[]{:S(2)}) copy-start(bf16[2,384,160]{1,2,0:T(8,128)(2,1)} %copy-done.6) | copy-start | bytes 737284
  102.2 20.7 %copy-start.5 = (bf16[2,384,160]{1,2,0:T(8,128)(2,1)S(1)}, bf16[2,384,160]{1,2,0:T(8,128)(2,1)}, u32[]{:S(2)}) copy-start(bf16[2,384,160]{1,2,0:T(8,128)(2,1)} %copy-done.4) | copy-start | bytes 737284
  102.2 20.8 %copy-start.3 = (bf16[2,384,160]{1,2,0:T(8,128)(2,1)S(1)}, bf16[2,384,160]{1,2,0:T(8,128)(2,1)}, u32[]{:S(2)}) copy-start(bf16[2,384,160]{1,2,0:T(8,128)(2,1)} %copy-done.2) | copy-start | bytes 737284
  120.8 125.0 %copy-start.10 = (f32[1280]{0:T(1024)S(1)}, f32[1280]{0:T(1024)}, u32[]{:S(2)}) copy-start(f32[1280]{0:T(1024)} %param.10) | copy-start | bytes 15364
  123.1 1.9 copy-start.1
Sparse Core Ops, SparseCore 0:
  9.5 132.2 all-gather.2
  144.0 101.7 all-gather.4
